TPU v7x, 128 devices: a whole 4x4x4 slice. The times are simulated.
128 devices in a mesh: section: 2 (over z_lo), dp: 8 (over y, core), tensor: 8 (over z_hi, x).
Axes of the slice: x: 4, y: 4, z: 4 (z_hi: 2, z_lo: 2; z = z_hi * 2 + z_lo), core: 2. Of those that a mesh axis runs over, the one named last changes fastest.
Arguments:
- inputs: bfloat16 [384, 8192], P('tensor', 'dp'), may hold values from -6 to 6
- cotangent: bfloat16 [384, 8192], P('tensor', 'dp'), may hold values from -1.5 to 1.5
- gate_weight: bfloat16 [2, 8192, 14336], P('section', 'dp', 'tensor'), may hold values from -0.0625 to 0.0625
- up_weight: bfloat16 [2, 8192, 14336], P('section', 'dp', 'tensor'), may hold values from -0.0625 to 0.0625
- down_weight: bfloat16 [2, 14336, 8192], P('section', 'tensor', 'dp'), may hold values from -0.046875 to 0.046875
Outputs:
- section_out: bfloat16 [2, 384, 8192], P('section', 'tensor', 'dp')
- input_grad: bfloat16 [2, 384, 8192], P('section', 'tensor', 'dp')
- gate_grad: bfloat16 [2, 8192, 14336], P('section', 'dp', 'tensor')
- up_grad: bfloat16 [2, 8192, 14336], P('section', 'dp', 'tensor')
- down_grad: bfloat16 [2, 14336, 8192], P('section', 'tensor', 'dp')
All inputs are finite; a program needn't handle non-finite values.
Results may differ from a plain program's by a relative error of at most 0.015.
Values may be sent and summed in bfloat16 or wider, within the bound.
A program may use at most 128 MiB of HBM per device.

v0:
```python
import jax
import jax.numpy as jnp
from jax import lax
from jax.experimental import pallas as pl
from jax.experimental.pallas import tpu as pltpu
from jax.sharding import PartitionSpec as P

MESH = pl.DeviceIdType.MESH
F32 = jnp.float32
BF16 = jnp.bfloat16

D = 1024
HID = 1792
HC = HID // 2
NQ = 3
RB = 16
TB = 2 * RB
HT = 4 * TB

BUFFERS = {
    "wg": ((D, HID), BF16),
    "wu": ((D, HID), BF16),
    "wd": ((HID, D), BF16),
    "wgt": ((HID, D), BF16),
    "wut": ((HID, D), BF16),
    "wdt": ((D, HID), BF16),
    "u": ((NQ, 4, 2, RB, D), BF16),
    "g": ((NQ, 4, 2, RB, D), BF16),
    "hid": ((NQ, 4, TB, HID), BF16),
    "grad": ((NQ, 4, 2, TB, HID), BF16),
    "fac": ((NQ, 4, 2, TB, HID), BF16),
    "gh": ((NQ, 4, TB, HID), BF16),
    "f_psend": ((NQ, 2, 4, TB, HC), BF16),
    "f_precv": ((NQ, 2, 4, TB, HC), BF16),
    "f_own": ((NQ, 2, 4, TB, HC), F32),
    "f_ysend": ((NQ, 3, 2, TB, HC), BF16),
    "f_yrecv": ((NQ, 3, 2, TB, HC), BF16),
    "b_psend": ((NQ, 1, 4, TB, HC), BF16),
    "b_precv": ((NQ, 1, 4, TB, HC), BF16),
    "b_own": ((NQ, 1, 4, TB, HC), F32),
    "b_ysend": ((NQ, 3, 1, TB, HC), BF16),
    "b_yrecv": ((NQ, 3, 1, TB, HC), BF16),
    "ghown": ((NQ, TB, HC), F32),
    "xsend": ((2, NQ, 4, 2, RB, D), BF16),
    "xrecv": ((2, NQ, 2, 4, RB, D), BF16),
    "res": ((NQ, RB, D), BF16),
    "home": ((NQ, RB, D), BF16),
}


def slot_table():
    names = []
    for h in range(NQ):
        names += [(p, h, z, k) for p in ("in", "next") for z in range(2) for k in range(4)]
        for p in ("f", "b"):
            names.append((p + "pair", h))
            names += [(p + "y", h, k) for k in (1, 2, 3)]
        for a in ("hid", "grad", "fac", "gh"):
            names += [(a + "y", h, k) for k in (1, 2, 3)]
            names += [(a + "p", h, k) for k in range(4)]
        names += [("x", tag, h, z, k) for tag in range(2) for z in range(2) for k in range(4)]
    names += [("home",)]
    return {name: i for i, name in enumerate(names)}


SLOTS = slot_table()

ALL = [(1, 2), (1, 1), (1, 3), (0, 2), (0, 1), (0, 3), (1, 0), (0, 0)]
OTHERS = ALL[:-1]


def each_tile(total, body, width=256, unroll=False):
    if unroll:
        for o in range(0, total, width):
            body(o, min(width, total - o))
        return

    def step(i, carry):
        body(pl.multiple_of(i * width, width), width)
        return carry

    lax.fori_loop(0, total // width, step, 0)
    if total % width:
        body(total - total % width, total % width)


def dot_nn(a, b):
    return lax.dot_general(a, b, (((1,), (0,)), ((), ())), preferred_element_type=F32)


def dot_nt(a, b):
    return lax.dot_general(a, b, (((1,), (1,)), ((), ())), preferred_element_type=F32)


def dot_tn(a, b):
    return lax.dot_general(a, b, (((0,), (0,)), ((), ())), preferred_element_type=F32)


def kernel(in_hbm, ct_hbm, wg_hbm, wu_hbm, wd_hbm, so_ref, ig_ref, og_ref, ou_ref, od_ref, *scratch):
    b = dict(zip(BUFFERS, scratch))
    send_sem, recv_sem, load_sem, go_sem = scratch[len(BUFFERS):]
    s, d, t = lax.axis_index("section"), lax.axis_index("dp"), lax.axis_index("tensor")
    y, c = d // 2, d % 2
    zh, x = t // 4, t % 4

    def ring(v, k):
        return (v + k) % 4

    def at_y(k):
        return {"dp": ring(y, k) * 2 + c}

    def z_hi(z):
        return zh if z == 0 else 1 - zh

    def at_x(z, k):
        return {"tensor": z_hi(z) * 4 + ring(x, k)}

    def at_next(z, k):
        return {"section": 1 - s, "tensor": z_hi(z) * 4 + ring(x, k)}

    pair = {"dp": y * 2 + 1 - c}
    same = {"section": 1 - s}
    col = pl.multiple_of(c * HC, 128)
    col_other = pl.multiple_of((1 - c) * HC, 128)

    barrier = pltpu.get_barrier_semaphore()
    peers = [pair] + [at_y(k) for k in (1, 2, 3)]
    peers += [at_x(z, k) for z, k in OTHERS] + [at_next(z, k) for z, k in ALL]
    for peer in peers:
        pl.semaphore_signal(barrier, 1, device_id=peer, device_id_type=MESH)
    weights = {}
    for i, (name, src) in enumerate((("wg", wg_hbm), ("wu", wu_hbm), ("wd", wd_hbm))):
        weights[name] = pltpu.make_async_copy(src.at[0], b[name], load_sem.at[i])
        weights[name].start()
    pl.semaphore_wait(barrier, len(peers))

    def role(first):
        sent = []
        residual = ct_hbm if first else in_hbm
        loads = []
        for h in range(NQ):
            loads.append(
                pltpu.make_async_copy(residual.at[pl.ds(h * RB, RB)], b["res"].at[h], load_sem.at[3 + h])
            )
            loads[-1].start()


        def send(slot, src, dst, peer):
            i = SLOTS[slot]
            copy = pltpu.make_async_remote_copy(
                src_ref=src, dst_ref=dst, send_sem=send_sem.at[i], recv_sem=recv_sem.at[i],
                device_id=peer, device_id_type=MESH,
            )
            copy.start()
            sent.append(copy)
            return copy

        def arrived(slot, dst):
            i = SLOTS[slot]
            pltpu.make_async_remote_copy(
                src_ref=dst, dst_ref=dst, send_sem=send_sem.at[i], recv_sem=recv_sem.at[i],
                device_id=pair, device_id_type=MESH,
            ).wait_recv()

        def gather(p, h, src, full):
            for z, k in OTHERS:
                send((p, h, z, k), src, full.at[h, x, zh], at_x(z, k))

        def gathered(p, h, full):
            for z, k in reversed(OTHERS):
                arrived((p, h, z, k), full.at[h, ring(x, 4 - k), z_hi(z)])

        def gather_input(src, full):
            for h in range(NQ):
                rows = src.at[pl.ds(h * RB, RB)]
                place = recv_sem.at[SLOTS[("in", h, 0, 0)]]
                pltpu.make_async_copy(rows, full.at[h, x, zh], place).start()
                gather("in", h, rows, full)

        def input_wait(h, full):
            arrived(("in", h, 0, 0), full.at[h, x, zh])
            gathered("in", h, full)

        def mm_forward(h):
            u = b["u"][h].reshape(HT, D)
            for dst, start in ((b["f_psend"], col_other), (b["f_own"], col)):
                def tile(o, n):
                    for a, w in enumerate((b["wg"], b["wu"])):
                        r = dot_nn(u, w[:, pl.ds(pl.multiple_of(start + o, 128), n)])
                        dst[h, a, :, :, pl.ds(o, n)] = r.reshape(4, TB, n).astype(dst.dtype)

                each_tile(HC, tile, unroll=True)
                if dst is b["f_psend"]:
                    send(("fpair", h), dst.at[h], b["f_precv"].at[h], pair)

        def mm_hidden(h):
            g = b["g"][h].reshape(HT, D)
            for dst, start in ((b["b_psend"], col_other), (b["b_own"], col)):
                def tile(o, n):
                    cols = pl.ds(pl.multiple_of(start + o, 128), n)
                    r = dot_nn(g, b["wdt"][:, cols]) if first else dot_nt(g, b["wd"][cols, :])
                    dst[h, 0, :, :, pl.ds(o, n)] = r.reshape(4, TB, n).astype(dst.dtype)

                each_tile(HC, tile, unroll=first)
                if dst is b["b_psend"]:
                    send(("bpair", h), dst.at[h], b["b_precv"].at[h], pair)

        def pair_add(p, h):
            own, prec, ysend = (b[p + n] for n in ("_own", "_precv", "_ysend"))
            arrived((p + "pair", h), prec.at[h])
            for k in (2, 1, 3):
                j = ring(y, k)
                for a in range(own.shape[1]):
                    ysend[h, k - 1, a] = (own[h, a, j] + prec[h, a, j].astype(F32)).astype(BF16)

        def y_scatter(p, h, ks=(2, 1, 3)):
            ysend, yrecv = b[p + "_ysend"], b[p + "_yrecv"]
            return [
                send((p + "y", h, k), ysend.at[h, k - 1], yrecv.at[h, k - 1], at_y(k)) for k in ks
            ]

        def y_sum(p, h):
            own, prec, yrecv = (b[p + n] for n in ("_own", "_precv", "_yrecv"))
            total = [own[h, a, y] + prec[h, a, y].astype(F32) for a in range(own.shape[1])]
            for k in (1, 3, 2):
                arrived((p + "y", h, k), yrecv.at[h, k - 1])
            for k in (1, 2, 3):
                total = [v + yrecv[h, k - 1, a].astype(F32) for a, v in enumerate(total)]
            return total

        def block(name, h, j, start):
            ref = b[name]
            cols = pl.ds(start, HC)
            return ref.at[h, j, :, :, cols] if len(ref.shape) == 5 else ref.at[h, j, :, cols]

        def spread(name, h):
            ref = block(name, h, y, col)
            copies = [send((name + "y", h, k), ref, ref, at_y(k)) for k in (2, 1, 3)]
            send((name + "p", h, 0), ref, ref, pair)
            return copies

        def forward_pair(name, h):
            for k in (1, 3, 2):
                ref = block(name, h, ring(y, 4 - k), col)
                arrived((name + "y", h, k), ref)
                send((name + "p", h, k), ref, ref, pair)

        def pair_wait(name, h):
            for k in (0, 1, 3, 2):
                arrived((name + "p", h, k), block(name, h, ring(y, 4 - k), col_other))

        def x_scatter(tag, h, term):
            def tile(o, n):
                r = term(pl.ds(o, n)).reshape(4, 2, RB, n)
                b["xsend"][tag, h, :, :, :, pl.ds(o, n)] = r.astype(BF16)

            each_tile(D, tile, unroll=first or tag == 0)
            for z, k in (ALL, OTHERS)[tag]:
                send(
                    ("x", tag, h, z, k), b["xsend"].at[tag, h, ring(x, k), z_hi(z)],
                    b["xrecv"].at[tag, h, z, k], (at_next, at_x)[tag](z, k),
                )

        def x_sum(tag, h, total):
            peers = (ALL, OTHERS)[tag]
            for z, k in reversed(peers):
                arrived(("x", tag, h, z, k), b["xrecv"].at[tag, h, z, k])
            for z, k in peers:
                total = total + b["xrecv"][tag, h, z, k].astype(F32)
            return total

        def down(tag, h):
            hid = b["hid"][h].reshape(HT, HID)
            x_scatter(tag, h, lambda cols: dot_nn(hid, b["wd"][:, cols]))

        def back(tag, h):
            gg = b["grad"][h, :, 0].reshape(HT, HID)
            gu = b["grad"][h, :, 1].reshape(HT, HID)
            x_scatter(tag, h, lambda cols: dot_nn(gg, b["wgt"][:, cols]) + dot_nn(gu, b["wut"][:, cols]))

        def from_other(h, dst):
            dst[h, x, zh] = x_sum(0, h, b["res"][h].astype(F32)).astype(BF16)
            gather("next", h, dst.at[h, x, zh], dst)

        def finish(h, residual, out_ref):
            total = residual[h, x, zh].astype(F32) + b["xsend"][1, h, x, zh].astype(F32)
            out_ref[0, h * RB:(h + 1) * RB] = x_sum(1, h, total).astype(BF16)

        def send_home(full):
            send(("home",), full.at[:, x, zh], b["home"], same)

        def home(out_ref):
            arrived(("home",), b["home"])
            out_ref[0] = b["home"][...].reshape(NQ * RB, D)

        def transpose(name):
            src, dst = b[name], b[name + "t"]
            def tile(o, n):
                dst[pl.ds(o, n), :] = src[:, pl.ds(o, n)].T

            each_tile(dst.shape[0], tile)

        def weight_grad(lhs, rhs, out):
            def tile(o, n):
                out[0, pl.ds(o, n), :] = dot_tn(lhs(o, n), rhs()).astype(BF16)

            each_tile(out.shape[1], tile)

        def down_grad():
            weight_grad(
                lambda o, n: b["hid"][:, :, :, pl.ds(o, n)].reshape(NQ * HT, n),
                lambda: b["g"][...].reshape(NQ * HT, D), od_ref,
            )

        def gate_grad(a):
            weight_grad(
                lambda o, n: b["u"][:, :, :, :, pl.ds(o, n)].reshape(NQ * HT, n),
                lambda: b["grad"][:, :, a].reshape(NQ * HT, HID),
                (og_ref, ou_ref)[a],
            )

        def act_first(h):
            gate, up = y_sum("f", h)
            sig = 1.0 / (1.0 + jnp.exp(-gate))
            b["hid"][h, y, :, pl.ds(col, HC)] = (gate * sig * up).astype(BF16)
            copies = spread("hid", h)
            b["fac"][h, y, 0, :, pl.ds(col, HC)] = (up * sig * (1.0 + gate * (1.0 - sig))).astype(BF16)
            b["fac"][h, y, 1, :, pl.ds(col, HC)] = (gate * sig).astype(BF16)
            return copies

        def act_second(h):
            gate, up = y_sum("f", h)
            sig = 1.0 / (1.0 + jnp.exp(-gate))
            gh = b["ghown"][h]
            grad_gate = gh * up * sig * (1.0 + gate * (1.0 - sig))
            b["grad"][h, y, 0, :, pl.ds(col, HC)] = grad_gate.astype(BF16)
            b["grad"][h, y, 1, :, pl.ds(col, HC)] = (gh * gate * sig).astype(BF16)
            copies = spread("grad", h)
            b["hid"][h, y, :, pl.ds(col, HC)] = (gate * sig * up).astype(BF16)
            return copies

        def spread_hidden_grad(h):
            (gh,) = y_sum("b", h)
            b["gh"][h, y, :, pl.ds(col, HC)] = gh.astype(BF16)
            spread("gh", h)

        def hidden_back(tag, h):
            pair_wait("gh", h)
            for j in range(4):
                gh = b["gh"][h, j].astype(F32)
                for a in range(2):
                    b["grad"][h, j, a] = (gh * b["fac"][h, j, a].astype(F32)).astype(BF16)
            back(tag, h)

        def out_of_features(p, h):
            pair_add(p, h)
            y_scatter(p, h)

        def down_next(h):
            pair_wait("hid", h)
            down(0, h)

        def back_next(h):
            pair_wait("grad", h)
            back(0, h)

        chunks = range(NQ)

        def run(order, steps):
            for word in order:
                steps[word[0]](int(word[1]))

        if first:
            gather_input(in_hbm, b["u"])
            weights["wg"].wait()
            weights["wu"].wait()

            def start(h):
                input_wait(h, b["u"])
                mm_forward(h)

            run([
                "a0", "a1", "b0", "a2", "b1", "c0", "b2", "s0", "w0", "c1",
                "d0", "e0", "d1", "c2", "e1", "d2", "e2",
            ], {
                "a": start,
                "b": lambda h: out_of_features("f", h),
                "c": act_first,
                "d": lambda h: forward_pair("hid", h),
                "e": down_next,
                "s": lambda h: pl.semaphore_signal(go_sem, 1, device_id=same, device_id_type=MESH),
                "w": lambda h: weights["wd"].wait(),
            })
            for h in chunks:
                spread("fac", h)
            for name in ("wg", "wu", "wd"):
                transpose(name)
            for h in chunks:
                forward_pair("fac", h)
            for h in chunks:
                pair_wait("fac", h)
            for copy in loads:
                copy.wait()
            run([
                "g0", "h0", "m0", "b0", "g1", "c0", "h1", "m1", "b1", "g2",
                "t0", "d0", "e0", "c1", "h2", "m2", "b2", "d1", "e1", "c2",
                "q0", "d2", "e2", "p0", "r0", "r1", "p1", "r2",
            ], {
                "g": lambda h: from_other(h, b["g"]),
                "h": lambda h: gathered("next", h, b["g"]),
                "m": mm_hidden,
                "b": lambda h: out_of_features("b", h),
                "c": spread_hidden_grad,
                "d": lambda h: forward_pair("gh", h),
                "e": lambda h: hidden_back(1, h),
                "t": lambda h: send_home(b["g"]),
                "q": lambda h: down_grad(),
                "p": gate_grad,
                "r": lambda h: finish(h, b["g"], ig_ref),
            })
            home(so_ref)
        else:
            weights["wg"].wait()
            weights["wu"].wait()
            transpose("wg")
            transpose("wu")
            pl.semaphore_wait(go_sem, 1)
            gather_input(ct_hbm, b["g"])
            weights["wd"].wait()
            for h in chunks:
                input_wait(h, b["g"])
                mm_hidden(h)
            for h in chunks:
                out_of_features("b", h)
            for h in chunks:
                (b["ghown"][h],) = y_sum("b", h)
            for copy in loads:
                copy.wait()
            run([
                "g0", "h0", "a0", "g1", "b0", "h1", "a1", "g2", "b1", "c0",
                "h2", "a2", "b2", "c1", "d0", "e0", "c2", "d1", "e1", "d2",
                "e2",
            ], {
                "g": lambda h: from_other(h, b["u"]),
                "h": lambda h: gathered("next", h, b["u"]),
                "a": mm_forward,
                "b": lambda h: out_of_features("f", h),
                "c": act_second,
                "d": lambda h: forward_pair("grad", h),
                "e": back_next,
            })
            send_home(b["u"])
            for h in chunks:
                spread("hid", h)
            for h in chunks:
                forward_pair("hid", h)
            for h in chunks:
                pair_wait("hid", h)
                down(1, h)
            gate_grad(0)
            gate_grad(1)
            down_grad()
            for h in chunks:
                finish(h, b["u"], so_ref)
            home(ig_ref)
        for copy in sent:
            copy.wait_send()

    pl.when(s == 0)(lambda: role(True))
    pl.when(s == 1)(lambda: role(False))


def write_out(*refs):
    sems = refs[-1]
    half = len(refs) // 2
    copies = []
    for src, dst in zip(refs[:half], refs[half:-1]):
        rows = src.shape[1]
        step = rows if rows < 1024 else rows // 4
        for o in range(0, rows, step):
            part = pl.ds(o, step)
            copies.append(pltpu.make_async_copy(src.at[:, part], dst.at[:, part], sems.at[len(copies)]))
            copies[-1].start()
    for copy in copies:
        copy.wait()


def per_device(inputs, cotangent, gate_weight, up_weight, down_weight):
    any_spec = pl.BlockSpec(memory_space=pl.ANY)
    vmem_spec = pl.BlockSpec(memory_space=pltpu.VMEM)
    n = len(SLOTS)
    shapes = [(1, NQ * RB, D), (1, NQ * RB, D), (1, D, HID), (1, D, HID), (1, HID, D)]
    outs = pl.pallas_call(
        kernel,
        out_shape=[pltpu.VMEM(shape, BF16) for shape in shapes],
        in_specs=[any_spec] * 5,
        out_specs=[vmem_spec] * 5,
        scratch_shapes=[pltpu.VMEM(shape, dtype) for shape, dtype in BUFFERS.values()]
        + [
            pltpu.SemaphoreType.DMA((n,)),
            pltpu.SemaphoreType.DMA((n,)),
            pltpu.SemaphoreType.DMA((3 + NQ,)),
            pltpu.SemaphoreType.REGULAR,
        ],
        compiler_params=pltpu.CompilerParams(
            collective_id=0, has_side_effects=True, vmem_limit_bytes=50 << 20
        ),
        name="sections",
    )(inputs, cotangent, gate_weight, up_weight, down_weight)
    return pl.pallas_call(
        write_out,
        out_shape=[jax.ShapeDtypeStruct(shape, BF16) for shape in shapes],
        in_specs=[vmem_spec] * 5,
        out_specs=[any_spec] * 5,
        scratch_shapes=[pltpu.SemaphoreType.DMA((14,))],
        compiler_params=pltpu.CompilerParams(vmem_limit_bytes=2 << 20),
        name="write_out",
    )(*outs)


def solution(mesh):
    in_specs = (
        P("tensor", "dp"),
        P("tensor", "dp"),
        P("section", "dp", "tensor"),
        P("section", "dp", "tensor"),
        P("section", "tensor", "dp"),
    )
    out_specs = (
        P("section", "tensor", "dp"),
        P("section", "tensor", "dp"),
        P("section", "dp", "tensor"),
        P("section", "dp", "tensor"),
        P("section", "tensor", "dp"),
    )
    return jax.shard_map(
        per_device, mesh=mesh, in_specs=in_specs, out_specs=out_specs, check_vma=False
    )
```

profile of v0, /device:TPU:1, one launch (start us, length us, event | category | flops | bytes accessed | tf_op | source)
XLA Modules:
  0.0 137.7 jit_solution(14177338262113907081)
XLA Ops:
  0.6 132.6 %sections.1 = (bf16[1,48,1024]{2,1,0:T(8,128)(2,1)S(1)}, bf16[1,48,1024]{2,1,0:T(8,128)(2,1)S(1)}, bf16[1,1024,1792]{2,1,0:T(8,128)(2,1)S(1)}, bf16[1,1024,1792]...) custom-call(bf16[48,1024]{1,0:T(8,128)(2,1)} %in_hbm.1, bf16[48,1024]{1,0:T(8,128)(2,1)} %ct_hbm.1, ...), custom_call_target="tpu_custom_call" | custom-call | tf_op jit(solution)/shard_map/sections/pallas_call | solution.py:493
  133.2 4.3 %write_out.1 = (bf16[1,48,1024]{2,1,0:T(8,128)(2,1)}, bf16[1,48,1024]{2,1,0:T(8,128)(2,1)}, bf16[1,1024,1792]{2,1,0:T(8,128)(2,1)}, bf16[1,1024,1792]{2,1,0:T(8,128)(2,1)}, bf16[1,1792,1024]{2,1,0:T(8,128)(2,1)}) custom-call(bf16[1,48,1024]{2,1,0:T(8,128)(2,1)S(1)} %get-tuple-element.10.refs_0_, bf16[1,48,1024]{2,1,0:T(8,128)(2,1)S(1)} %get-tuple-element.11.refs_1_, ...), custom_call_target="tpu_custom_call" | custom-call | tf_op jit(solution)/shard_map/write_out/pallas_call | solution.py:510
where the time goes:
time: 138 us
  Pallas kernels  137 us (99%)
    pallas_call x1, Pallas kernels, per_device(): pl.pallas_call(kernel, out_shape=[pltpu.VMEM(shape, BF16) for shape in sh...  133 us
    pallas_call x1, Pallas kernels, per_device(): pl.pallas_call(write_out, out_shape=[jax.ShapeDtypeStruct(shape, BF16) fo...  4.28 us

commit v1 on v0

--- a/solution.py
+++ b/solution.py
@@ -40,10 +40,10 @@
     "b_own": ((NQ, 1, 4, TB, HC), F32),
     "b_ysend": ((NQ, 3, 1, TB, HC), BF16),
     "b_yrecv": ((NQ, 3, 1, TB, HC), BF16),
-    "ghown": ((NQ, TB, HC), F32),
     "xsend": ((2, NQ, 4, 2, RB, D), BF16),
     "xrecv": ((2, NQ, 2, 4, RB, D), BF16),
     "res": ((NQ, RB, D), BF16),
+    "acc": ((HT, D), F32),
     "home": ((NQ, RB, D), BF16),
 }
 
@@ -58,7 +58,10 @@
         for a in ("hid", "grad", "fac", "gh"):
             names += [(a + "y", h, k) for k in (1, 2, 3)]
             names += [(a + "p", h, k) for k in range(4)]
-        names += [("x", tag, h, z, k) for tag in range(2) for z in range(2) for k in range(4)]
+        names += [
+            ("x", tag, h, z, k, part)
+            for tag in range(2) for z in range(2) for k in range(4) for part in range(2)
+        ]
     names += [("home",)]
     return {name: i for i, name in enumerate(names)}
 
@@ -205,19 +208,14 @@
                 if dst is b["b_psend"]:
                     send(("bpair", h), dst.at[h], b["b_precv"].at[h], pair)
 
-        def pair_add(p, h):
-            own, prec, ysend = (b[p + n] for n in ("_own", "_precv", "_ysend"))
+        def out_of_features(p, h):
+            own, prec, ysend, yrecv = (b[p + n] for n in ("_own", "_precv", "_ysend", "_yrecv"))
             arrived((p + "pair", h), prec.at[h])
             for k in (2, 1, 3):
                 j = ring(y, k)
                 for a in range(own.shape[1]):
                     ysend[h, k - 1, a] = (own[h, a, j] + prec[h, a, j].astype(F32)).astype(BF16)
-
-        def y_scatter(p, h, ks=(2, 1, 3)):
-            ysend, yrecv = b[p + "_ysend"], b[p + "_yrecv"]
-            return [
-                send((p + "y", h, k), ysend.at[h, k - 1], yrecv.at[h, k - 1], at_y(k)) for k in ks
-            ]
+                send((p + "y", h, k), ysend.at[h, k - 1], yrecv.at[h, k - 1], at_y(k))
 
         def y_sum(p, h):
             own, prec, yrecv = (b[p + n] for n in ("_own", "_precv", "_yrecv"))
@@ -254,29 +252,51 @@
                 r = term(pl.ds(o, n)).reshape(4, 2, RB, n)
                 b["xsend"][tag, h, :, :, :, pl.ds(o, n)] = r.astype(BF16)
 
-            each_tile(D, tile, unroll=first or tag == 0)
-            for z, k in (ALL, OTHERS)[tag]:
-                send(
-                    ("x", tag, h, z, k), b["xsend"].at[tag, h, ring(x, k), z_hi(z)],
-                    b["xrecv"].at[tag, h, z, k], (at_next, at_x)[tag](z, k),
-                )
+            for part in range(2):
+                start = part * (D // 2)
+                each_tile(D // 2, lambda o, n: tile(start + o, n), unroll=first or tag == 0)
+                cols = pl.ds(start, D // 2)
+                for z, k in (ALL, OTHERS)[tag]:
+                    send(
+                        ("x", tag, h, z, k, part), b["xsend"].at[tag, h, ring(x, k), z_hi(z), :, cols],
+                        b["xrecv"].at[tag, h, z, k, :, cols], (at_next, at_x)[tag](z, k),
+                    )
 
         def x_sum(tag, h, total):
             peers = (ALL, OTHERS)[tag]
-            for z, k in reversed(peers):
-                arrived(("x", tag, h, z, k), b["xrecv"].at[tag, h, z, k])
+            for part in range(2):
+                cols = pl.ds(part * (D // 2), D // 2)
+                for z, k in reversed(peers):
+                    arrived(("x", tag, h, z, k, part), b["xrecv"].at[tag, h, z, k, :, cols])
             for z, k in peers:
                 total = total + b["xrecv"][tag, h, z, k].astype(F32)
             return total
 
+        def over_hidden(tag, h, name, term):
+            own, other = pl.ds(col, HC), pl.ds(col_other, HC)
+
+            def tile(o, n):
+                b["acc"][:, pl.ds(o, n)] = term(own, pl.ds(o, n))
+
+            each_tile(D, tile, unroll=first or tag == 0)
+            pair_wait(name, h)
+            return lambda cols: b["acc"][:, cols] + term(other, cols)
+
         def down(tag, h):
-            hid = b["hid"][h].reshape(HT, HID)
-            x_scatter(tag, h, lambda cols: dot_nn(hid, b["wd"][:, cols]))
-
-        def back(tag, h):
-            gg = b["grad"][h, :, 0].reshape(HT, HID)
-            gu = b["grad"][h, :, 1].reshape(HT, HID)
-            x_scatter(tag, h, lambda cols: dot_nn(gg, b["wgt"][:, cols]) + dot_nn(gu, b["wut"][:, cols]))
+            x_scatter(tag, h, over_hidden(tag, h, "hid", lambda part, cols: dot_nn(
+                b["hid"][h, :, :, part].reshape(HT, HC), b["wd"][part, cols]
+            )))
+
+        def back(tag, h, name):
+            def term(part, cols):
+                gg = b["grad"][h, :, 0, :, part].reshape(HT, HC)
+                gu = b["grad"][h, :, 1, :, part].reshape(HT, HC)
+                return dot_nn(gg, b["wgt"][part, cols]) + dot_nn(gu, b["wut"][part, cols])
+
+            later = over_hidden(tag, h, name, term)
+            if first:
+                hidden_grads(h, col_other)
+            x_scatter(tag, h, later)
 
         def from_other(h, dst):
             dst[h, x, zh] = x_sum(0, h, b["res"][h].astype(F32)).astype(BF16)
@@ -329,9 +349,9 @@
             return copies
 
         def act_second(h):
+            (gh,) = y_sum("b", h)
             gate, up = y_sum("f", h)
             sig = 1.0 / (1.0 + jnp.exp(-gate))
-            gh = b["ghown"][h]
             grad_gate = gh * up * sig * (1.0 + gate * (1.0 - sig))
             b["grad"][h, y, 0, :, pl.ds(col, HC)] = grad_gate.astype(BF16)
             b["grad"][h, y, 1, :, pl.ds(col, HC)] = (gh * gate * sig).astype(BF16)
@@ -344,25 +364,16 @@
             b["gh"][h, y, :, pl.ds(col, HC)] = gh.astype(BF16)
             spread("gh", h)
 
+        def hidden_grads(h, start):
+            cols = pl.ds(start, HC)
+            for j in range(4):
+                gh = b["gh"][h, j, :, cols].astype(F32)
+                for a in range(2):
+                    b["grad"][h, j, a, :, cols] = (gh * b["fac"][h, j, a, :, cols].astype(F32)).astype(BF16)
+
         def hidden_back(tag, h):
-            pair_wait("gh", h)
-            for j in range(4):
-                gh = b["gh"][h, j].astype(F32)
-                for a in range(2):
-                    b["grad"][h, j, a] = (gh * b["fac"][h, j, a].astype(F32)).astype(BF16)
-            back(tag, h)
-
-        def out_of_features(p, h):
-            pair_add(p, h)
-            y_scatter(p, h)
-
-        def down_next(h):
-            pair_wait("hid", h)
-            down(0, h)
-
-        def back_next(h):
-            pair_wait("grad", h)
-            back(0, h)
+            hidden_grads(h, col)
+            back(tag, h, "gh")
 
         chunks = range(NQ)
 
@@ -380,14 +391,14 @@
                 mm_forward(h)
 
             run([
-                "a0", "a1", "b0", "a2", "b1", "c0", "b2", "s0", "w0", "c1",
+                "a0", "b0", "a1", "b1", "a2", "s0", "c0", "b2", "w0", "c1",
                 "d0", "e0", "d1", "c2", "e1", "d2", "e2",
             ], {
                 "a": start,
                 "b": lambda h: out_of_features("f", h),
                 "c": act_first,
                 "d": lambda h: forward_pair("hid", h),
-                "e": down_next,
+                "e": lambda h: down(0, h),
                 "s": lambda h: pl.semaphore_signal(go_sem, 1, device_id=same, device_id_type=MESH),
                 "w": lambda h: weights["wd"].wait(),
             })
@@ -432,8 +443,6 @@
                 mm_hidden(h)
             for h in chunks:
                 out_of_features("b", h)
-            for h in chunks:
-                (b["ghown"][h],) = y_sum("b", h)
             for copy in loads:
                 copy.wait()
             run([
@@ -447,7 +456,7 @@
                 "b": lambda h: out_of_features("f", h),
                 "c": act_second,
                 "d": lambda h: forward_pair("grad", h),
-                "e": back_next,
+                "e": lambda h: back(0, h, "grad"),
             })
             send_home(b["u"])
             for h in chunks:
@@ -455,7 +464,6 @@
             for h in chunks:
                 forward_pair("hid", h)
             for h in chunks:
-                pair_wait("hid", h)
                 down(1, h)
             gate_grad(0)
             gate_grad(1)

time: 138 us -> 131 us (0.949)
  Pallas kernels: 137 us -> 130 us
    pallas_call x1, Pallas kernels: 133 us -> 125 us  [per_device(): pl.pallas_call(kernel, out_shape=[pltpu.VMEM(shape, BF16) for shape in sh...]
where the time goes in v1:
time: 131 us; the launch traced here: 130 us
  Pallas kernels  130 us (99%)
    pallas_call x1, Pallas kernels, per_device(): pl.pallas_call(kernel, out_shape=[pltpu.VMEM(shape, BF16) for shape in sh...  125 us
    pallas_call x1, Pallas kernels, per_device(): pl.pallas_call(write_out, out_shape=[jax.ShapeDtypeStruct(shape, BF16) fo...  4.28 us

profile of v1, /device:TPU:1, one launch (start us, length us, event | category | flops | bytes accessed | tf_op | source)
XLA Modules:
  0.0 130.5 jit_solution(11623186137755553587)
XLA Ops:
  0.6 125.4 %sections.1 = (bf16[1,48,1024]{2,1,0:T(8,128)(2,1)S(1)}, bf16[1,48,1024]{2,1,0:T(8,128)(2,1)S(1)}, bf16[1,1024,1792]{2,1,0:T(8,128)(2,1)S(1)}, bf16[1,1024,1792]...) custom-call(bf16[48,1024]{1,0:T(8,128)(2,1)} %in_hbm.1, bf16[48,1024]{1,0:T(8,128)(2,1)} %ct_hbm.1, ...), custom_call_target="tpu_custom_call" | custom-call | tf_op jit(solution)/shard_map/sections/pallas_call | solution.py:501
  126.0 4.3 %write_out.1 = (bf16[1,48,1024]{2,1,0:T(8,128)(2,1)}, bf16[1,48,1024]{2,1,0:T(8,128)(2,1)}, bf16[1,1024,1792]{2,1,0:T(8,128)(2,1)}, bf16[1,1024,1792]{2,1,0:T(8,128)(2,1)}, bf16[1,1792,1024]{2,1,0:T(8,128)(2,1)}) custom-call(bf16[1,48,1024]{2,1,0:T(8,128)(2,1)S(1)} %get-tuple-element.10.refs_0_, bf16[1,48,1024]{2,1,0:T(8,128)(2,1)S(1)} %get-tuple-element.11.refs_1_, ...), custom_call_target="tpu_custom_call" | custom-call | tf_op jit(solution)/shard_map/write_out/pallas_call | solution.py:518

commit v2 on v1

--- a/solution.py
+++ b/solution.py
@@ -51,7 +51,8 @@
 def slot_table():
     names = []
     for h in range(NQ):
-        names += [(p, h, z, k) for p in ("in", "next") for z in range(2) for k in range(4)]
+        names += [("in", h, z, k) for z in range(2) for k in range(4)]
+        names += [("next", h, z, k, part) for z in range(2) for k in range(4) for part in range(2)]
         for p in ("f", "b"):
             names.append((p + "pair", h))
             names += [(p + "y", h, k) for k in (1, 2, 3)]
@@ -262,14 +263,13 @@
                         b["xrecv"].at[tag, h, z, k, :, cols], (at_next, at_x)[tag](z, k),
                     )
 
-        def x_sum(tag, h, total):
+        def x_sum(tag, h, total, part):
             peers = (ALL, OTHERS)[tag]
-            for part in range(2):
-                cols = pl.ds(part * (D // 2), D // 2)
-                for z, k in reversed(peers):
-                    arrived(("x", tag, h, z, k, part), b["xrecv"].at[tag, h, z, k, :, cols])
+            cols = pl.ds(part * (D // 2), D // 2)
+            for z, k in reversed(peers):
+                arrived(("x", tag, h, z, k, part), b["xrecv"].at[tag, h, z, k, :, cols])
             for z, k in peers:
-                total = total + b["xrecv"][tag, h, z, k].astype(F32)
+                total = total + b["xrecv"][tag, h, z, k, :, cols].astype(F32)
             return total
 
         def over_hidden(tag, h, name, term):
@@ -299,12 +299,24 @@
             x_scatter(tag, h, later)
 
         def from_other(h, dst):
-            dst[h, x, zh] = x_sum(0, h, b["res"][h].astype(F32)).astype(BF16)
-            gather("next", h, dst.at[h, x, zh], dst)
+            for part in range(2):
+                cols = pl.ds(part * (D // 2), D // 2)
+                own = dst.at[h, x, zh, :, cols]
+                own[...] = x_sum(0, h, b["res"][h, :, cols].astype(F32), part).astype(BF16)
+                for z, k in OTHERS:
+                    send(("next", h, z, k, part), own, own, at_x(z, k))
+
+        def next_wait(h, full):
+            for part in range(2):
+                cols = pl.ds(part * (D // 2), D // 2)
+                for z, k in reversed(OTHERS):
+                    arrived(("next", h, z, k, part), full.at[h, ring(x, 4 - k), z_hi(z), :, cols])
 
         def finish(h, residual, out_ref):
-            total = residual[h, x, zh].astype(F32) + b["xsend"][1, h, x, zh].astype(F32)
-            out_ref[0, h * RB:(h + 1) * RB] = x_sum(1, h, total).astype(BF16)
+            for part in range(2):
+                cols = pl.ds(part * (D // 2), D // 2)
+                total = residual[h, x, zh, :, cols].astype(F32) + b["xsend"][1, h, x, zh, :, cols].astype(F32)
+                out_ref[0, h * RB:(h + 1) * RB, cols] = x_sum(1, h, total, part).astype(BF16)
 
         def send_home(full):
             send(("home",), full.at[:, x, zh], b["home"], same)
@@ -418,7 +430,7 @@
                 "q0", "d2", "e2", "p0", "r0", "r1", "p1", "r2",
             ], {
                 "g": lambda h: from_other(h, b["g"]),
-                "h": lambda h: gathered("next", h, b["g"]),
+                "h": lambda h: next_wait(h, b["g"]),
                 "m": mm_hidden,
                 "b": lambda h: out_of_features("b", h),
                 "c": spread_hidden_grad,
@@ -451,7 +463,7 @@
                 "e2",
             ], {
                 "g": lambda h: from_other(h, b["u"]),
-                "h": lambda h: gathered("next", h, b["u"]),
+                "h": lambda h: next_wait(h, b["u"]),
                 "a": mm_forward,
                 "b": lambda h: out_of_features("f", h),
                 "c": act_second,

time: 131 us -> 130 us (level)
  no operation moved by 1% of the time
where the time goes in v2:
time: 130 us
  Pallas kernels  129 us (99%)
    pallas_call x1, Pallas kernels, per_device(): pl.pallas_call(kernel, out_shape=[pltpu.VMEM(shape, BF16) for shape in sh...  125 us
    pallas_call x1, Pallas kernels, per_device(): pl.pallas_call(write_out, out_shape=[jax.ShapeDtypeStruct(shape, BF16) fo...  4.28 us

profile of v2, /device:TPU:1, one launch (start us, length us, event | category | flops | bytes accessed | tf_op | source)
XLA Modules:
  0.0 130.2 jit_solution(16458994108752380065)
XLA Ops:
  0.6 125.1 %sections.1 = (bf16[1,48,1024]{2,1,0:T(8,128)(2,1)S(1)}, bf16[1,48,1024]{2,1,0:T(8,128)(2,1)S(1)}, bf16[1,1024,1792]{2,1,0:T(8,128)(2,1)S(1)}, bf16[1,1024,1792]...) custom-call(bf16[48,1024]{1,0:T(8,128)(2,1)} %in_hbm.1, bf16[48,1024]{1,0:T(8,128)(2,1)} %ct_hbm.1, ...), custom_call_target="tpu_custom_call" | custom-call | tf_op jit(solution)/shard_map/sections/pallas_call | solution.py:513
  125.7 4.3 %write_out.1 = (bf16[1,48,1024]{2,1,0:T(8,128)(2,1)}, bf16[1,48,1024]{2,1,0:T(8,128)(2,1)}, bf16[1,1024,1792]{2,1,0:T(8,128)(2,1)}, bf16[1,1024,1792]{2,1,0:T(8,128)(2,1)}, bf16[1,1792,1024]{2,1,0:T(8,128)(2,1)}) custom-call(bf16[1,48,1024]{2,1,0:T(8,128)(2,1)S(1)} %get-tuple-element.10.refs_0_, bf16[1,48,1024]{2,1,0:T(8,128)(2,1)S(1)} %get-tuple-element.11.refs_1_, ...), custom_call_target="tpu_custom_call" | custom-call | tf_op jit(solution)/shard_map/write_out/pallas_call | solution.py:530
